TPU v7x, 512 devices: a whole 4x4x16 slice. The times are simulated.
512 devices in a mesh: dp: 64 (over y, z), segment: 2 (over core), mp: 4 (over x).
Axes of the slice: x: 4, y: 4, z: 16, core: 2. Of those that a mesh axis runs over, the one named last changes fastest.
Arguments:
- hidden: bfloat16 [2, 512, 4096], P('segment', ('dp', 'mp')), may hold values from -6 to 6
- gain: float32 [4096], replicated, may hold values from 0.5 to 1.5
- head: bfloat16 [4096, 131072], P('segment', ('dp', 'mp')), may hold values from -0.09375 to 0.09375
- queries: bfloat16 [8, 131072], P(None, ('dp', 'mp')), may hold values from -48 to 48
- doc_spans: int32 [8], replicated, may hold values from 1 to 4, as said below
- labels: int32 [8], replicated, may hold values from 0 to 7
Outputs:
- grad_head: bfloat16 [4096, 131072], P('segment', ('dp', 'mp'))
- loss: float32 [], replicated
Inputs may be any that keep to these rules, and one draw needn't show every extreme that they name: `doc_spans`: the counts sum to 16; documents own consecutive spans in order; at least two documents have 4 spans.
All inputs are finite; a program needn't handle non-finite values.
Results may differ from a plain program's by a relative error of at most 0.008.
Values may be sent and summed in bfloat16 or wider, within the bound.
A program may use at most 64 MiB of HBM per device.

v0:
```python
import math
import jax
import jax.numpy as jnp
from jax import lax
from jax.sharding import PartitionSpec as P

V_DEV = 512
CH_MB = 8
NDOC = 8


def saturate(logits):
    return jnp.log1p(jax.nn.softplus(logits))


def slope(logits):
    return jax.nn.sigmoid(logits) / (1.0 + jax.nn.softplus(logits))


def row_norm(hidden, gain):
    values = hidden.astype(jnp.float32)
    mean_sq = jnp.mean(values * values, axis=-1, keepdims=True)
    return (values * lax.rsqrt(mean_sq + 1e-05) * gain).astype(jnp.bfloat16)


def owned_by(span_ids, bounds):
    inside = (span_ids[:, None] >= bounds[None, :-1]) & (span_ids[:, None] < bounds[None, 1:])
    return inside.astype(jnp.float32)


def shards(hidden, gain, head, queries, doc_spans, labels):
    width_dp = lax.axis_size("dp")
    width_mp = lax.axis_size("mp")
    segments = lax.axis_size("segment")
    vocab = V_DEV * width_dp * width_mp
    rows_here = hidden.shape[1]
    tok_mb = rows_here * width_dp * width_mp
    span = tok_mb // CH_MB
    micro_index = lax.axis_index("segment")
    normed = row_norm(hidden, gain)
    head_full = lax.all_gather(head, "segment", axis=0, tiled=True)
    bounds = jnp.concatenate([jnp.zeros((1,), jnp.int32), jnp.cumsum(doc_spans)])
    query_values = queries.astype(jnp.float32)
    scale = 1.0 / (math.sqrt(vocab) * span)

    def doc_table(count):
        span_ids = (micro_index * tok_mb + jnp.arange(count, dtype=jnp.int32)) // span
        return owned_by(span_ids, bounds)

    table = doc_table(tok_mb)
    rows = lax.all_gather(normed, ("dp", "mp"), axis=1, tiled=True)[0]
    block = jnp.dot(rows, head_full, preferred_element_type=jnp.float32)
    local_table = doc_table(rows.shape[0])
    pooled_now = jnp.dot(local_table.T, saturate(block), precision=lax.Precision.HIGHEST)
    pooled = pooled_now
    pooled = lax.psum(pooled, "segment")
    terms = jnp.dot(query_values, pooled.T, precision=lax.Precision.HIGHEST)
    scores = lax.psum(terms, ("dp", "mp")) * scale
    row_top = jnp.max(scores, axis=1, keepdims=True)
    log_total = row_top + jnp.log(jnp.sum(jnp.exp(scores - row_top), axis=1, keepdims=True))
    picks = (labels[:, None] == jnp.arange(NDOC, dtype=jnp.int32)[None, :]).astype(jnp.float32)
    loss = jnp.sum(log_total[:, 0] - jnp.sum(scores * picks, axis=1))
    score_grad = jnp.exp(scores - log_total) - picks
    pooled_grad = scale * jnp.dot(score_grad.T, query_values, precision=lax.Precision.HIGHEST)
    token_grad = jnp.dot(table, pooled_grad, precision=lax.Precision.HIGHEST)
    grad_scale = math.sqrt(vocab) * span / math.sqrt(segments * tok_mb)
    logit_grad = (token_grad * slope(block) * grad_scale).astype(jnp.bfloat16)
    rows = lax.all_gather(normed, ("dp", "mp"), axis=1, tiled=True)[0]
    summed = lax.dot_general(
        rows, logit_grad, (((0,), (0,)), ((), ())), preferred_element_type=jnp.float32
    )
    grad_head = lax.psum_scatter(
        summed.astype(jnp.bfloat16), "segment", scatter_dimension=0, tiled=True
    )
    return (grad_head, loss)


def solution(mesh):
    return jax.shard_map(
        shards,
        mesh=mesh,
        in_specs=(
            P("segment", ("dp", "mp"), None),
            P(),
            P("segment", ("dp", "mp")),
            P(None, ("dp", "mp")),
            P(),
            P(),
        ),
        out_specs=(P("segment", ("dp", "mp")), P()),
        check_vma=False,
    )
```

profile of v0, /device:TPU:1, one launch (start us, length us, event | category | flops | bytes accessed | tf_op | source)
XLA Modules:
  0.0 1000.5 jit_solution(7330918718881482748)
XLA Ops:
  7.2 0.0 copy-start
  7.2 0.0 all-gather.5.cloned.1.call-start
  7.2 0.7 all-gather.5.cloned.1.call-update
  7.9 0.0 all-gather.3.cloned.1.call-start
  8.0 0.9 fusion.16
  8.8 0.8 fusion.18
  9.7 0.6 copy.10
  10.3 0.0 all-gather.3.cloned.1.call-update
  10.3 0.0 reduce-scatter.2.cloned.1.call-start
  10.4 0.8 reduce-window.8
  11.2 0.1 pad_add_fusion
  11.3 0.0 copy-start.1
  11.3 29.7 %all-gather.5.cloned.1.call-done = bf16[4096,512]{1,0:T(8,128)(2,1)} async-done(((bf16[2048,512]{1,0:T(8,128)(2,1)}), bf16[4096,512]{1,0:T(8,128)(2,1)}) %all-gather.5.cloned.1.call-update) | async-done | bytes 4194320 | tf_op jit(solution)/shard_map/all_gather | solution.py:41
  41.0 216.8 %all-gather.3.cloned.1.call-done = bf16[1,512,4096]{2,0,1:T(2,128)(2,1)} async-done(((bf16[1,2,4096]{2,0,1:T(2,128)(2,1)}), bf16[1,512,4096]{2,0,1:T(2,128)(2,1)}) %all-gather.3.cloned.1.call-update) | async-done | bytes 4194320 | tf_op jit(solution)/shard_map/all_gather | solution.py:68
  257.8 9.3 fusion.1
  267.1 1.4 fusion.7
  268.5 11.3 %psum.14 = f32[8,512]{1,0:T(8,128)S(1)} all-reduce(f32[8,512]{1,0:T(8,128)S(1)} %fusion.7), channel_id=1, replica_groups=mesh['dp'=64,'segment'=2,'mp'=4] {'segment'}, use_global_device_ids=true, to_apply=%region_2.3 | all-reduce | flops 4096 | bytes 32768 | tf_op jit(solution)/shard_map/psum | solution.py:56
  279.7 0.0 copy-done
  279.7 0.1 convolution_bitcast_fusion
  279.9 577.1 %psum.15 = f32[8,8]{0,1:T(8,128)S(1)} all-reduce(f32[8,8]{0,1:T(8,128)S(1)} %convolution_bitcast_fusion), channel_id=1, replica_groups=mesh['dp'=64,'segment'=2,'mp'=4] {'dp','mp'}, use_global_device_ids=true, to_apply=%region_3.4 | all-reduce | flops 64 | bytes 512 | tf_op jit(solution)/shard_map/psum | solution.py:58
  857.0 0.0 copy-done.1
  857.0 0.6 subtract_reduce_fusion
  857.6 0.1 convolution_multiply_fusion.1
  857.7 1.4 fusion.6
  859.1 14.9 %convolution_convert_fusion = bf16[4096,512]{1,0:T(8,128)(2,1)} fusion(bf16[512,512]{1,0:T(8,128)(2,1)S(1)} %fusion.6, bf16[1,512,4096]{2,0,1:T(2,128)(2,1)} %all-gather.3.cloned.1.call-done), kind=kOutput, calls=%fused_computation | convolution fusion | flops 2149580800 | bytes 8912896 | tf_op jit(solution)/shard_map/dot_general | solution.py:69
  874.0 0.0 reduce-scatter.2.cloned.1.call-update
  874.0 119.9 %reduce-scatter.2.cloned.1.call-done = bf16[2048,512]{1,0:T(8,128)(2,1)} async-done(((bf16[4096,512]{1,0:T(8,128)(2,1)}), bf16[2048,512]{1,0:T(8,128)(2,1)}) %reduce-scatter.2.cloned.1.call-update) | async-done | bytes 2097168 | tf_op jit(solution)/shard_map/reduce_scatter | solution.py:72
  (4 shorter events, 0.1 us)
Async XLA Ops:
  7.2 272.6 %copy-start = (bf16[8,512]{1,0:T(8,128)(2,1)S(1)}, bf16[8,512]{1,0:T(8,128)(2,1)}, u32[]{:S(2)}) copy-start(bf16[8,512]{1,0:T(8,128)(2,1)} %param.9) | copy-start | bytes 24580
  7.2 33.8 %all-gather.5.cloned.1.call-start = ((), (), s32[]{:S(2)}) async-start(), calls=%async_computation.2 | async-start | bytes 6291456 | tf_op jit(solution)/shard_map/all_gather | solution.py:41
  7.9 249.9 %all-gather.3.cloned.1.call-start = ((), (), s32[]{:S(2)}) async-start(), calls=%async_computation.1 | async-start | bytes 8421376 | tf_op jit(solution)/shard_map/all_gather | solution.py:68
  10.3 983.7 %reduce-scatter.2.cloned.1.call-start = ((), (), s32[]{:S(2)}) async-start(), calls=%async_computation.3 | async-start | bytes 6291456 | tf_op jit(solution)/shard_map/reduce_scatter | solution.py:72
  11.3 845.7 %copy-start.1 = (s32[8]{0:T(128)S(1)}, s32[8]{0:T(128)}, u32[]{:S(2)}) copy-start(s32[8]{0:T(128)} %param.11) | copy-start | bytes 100
Sparse Core Ops, SparseCore 0:
  10.1 30.8 all-gather.4
  46.2 211.6 all-gather.2
  874.2 119.7 reduce-scatter.1
where the time goes:
time: 1000 us
  blocking collectives  588 us (59%)
  waiting for transfers between devices  367 us (37%)
  matrix products  27.1 us (3%)
  between operations  13.8 us (1%)
    psum x1, blocking collectives, shards(): scores = lax.psum(terms, ('dp', 'mp')) * scale  577 us
    all_gather x1, waiting for transfers between devices, shards(): rows = lax.all_gather(normed, ('dp', 'mp'), axis=1, tiled=True)[0]  217 us
    reduce_scatter x1, waiting for transfers between devices, shards(): lax.psum_scatter(summed.astype(jnp.bfloat16), 'segment', scatter_dimensio...  120 us
    all_gather x1, waiting for transfers between devices, shards(): head_full = lax.all_gather(head, 'segment', axis=0, tiled=True)  29.7 us
  transfers between devices with their start and end apart: 3, of which 3 were waited for; matrix products, arithmetic and copies ran while one was open for 0% of the time, Pallas kernels for 0%

commit v1 on v0

--- a/solution.py
+++ b/solution.py
@@ -55,7 +55,7 @@
     pooled = pooled_now
     pooled = lax.psum(pooled, "segment")
     terms = jnp.dot(query_values, pooled.T, precision=lax.Precision.HIGHEST)
-    scores = lax.psum(terms, ("dp", "mp")) * scale
+    scores = lax.psum(lax.psum(terms, "dp"), "mp") * scale
     row_top = jnp.max(scores, axis=1, keepdims=True)
     log_total = row_top + jnp.log(jnp.sum(jnp.exp(scores - row_top), axis=1, keepdims=True))
     picks = (labels[:, None] == jnp.arange(NDOC, dtype=jnp.int32)[None, :]).astype(jnp.float32)

time: 1000 us -> 465 us (0.47)
  blocking collectives: 588 us -> 133 us
  waiting for transfers between devices: 367 us -> 287 us
    psum x1 -> x2, blocking collectives: 577 us -> 121 us  [shards(): scores = lax.psum(lax.psum(terms, 'dp'), 'mp') * scale]
    reduce_scatter x1, waiting for transfers between devices: 120 us -> 40 us  [shards(): lax.psum_scatter(summed.astype(jnp.bfloat16), 'segment', scatter_dimensio...]
  transfers between devices with their start and end apart: 3 -> 3, of which waited for: 3 -> 3; matrix products, arithmetic and copies ran while one was open for 0% -> 1% of each run, Pallas kernels for 0% -> 0%
where the time goes in v1:
time: 465 us
  waiting for transfers between devices  287 us (62%)
  blocking collectives  133 us (29%)
  matrix products  27.1 us (6%)
  between operations  13.8 us (3%)
    all_gather x1, waiting for transfers between devices, shards(): rows = lax.all_gather(normed, ('dp', 'mp'), axis=1, tiled=True)[0]  217 us
    psum x2, blocking collectives, shards(): scores = lax.psum(lax.psum(terms, 'dp'), 'mp') * scale  121 us
    reduce_scatter x1, waiting for transfers between devices, shards(): lax.psum_scatter(summed.astype(jnp.bfloat16), 'segment', scatter_dimensio...  40 us
    all_gather x1, waiting for transfers between devices, shards(): head_full = lax.all_gather(head, 'segment', axis=0, tiled=True)  29.7 us
    dot_general x1, matrix products, shards(): lax.dot_general(rows, logit_grad, (((0,), (0,)), ((), ())), preferred_ele...  14.9 us
    psum x1, blocking collectives, shards(): pooled = lax.psum(pooled, 'segment')  11.3 us
  transfers between devices with their start and end apart: 3, of which 3 were waited for; matrix products, arithmetic and copies ran while one was open for 1% of the time, Pallas kernels for 0%

profile of v1, /device:TPU:1, one launch (start us, length us, event | category | flops | bytes accessed | tf_op | source)
XLA Modules:
  0.0 464.9 jit_solution(7281263343579018955)
XLA Ops:
  7.2 0.0 copy-start
  7.2 0.0 all-gather.5.cloned.1.call-start
  7.2 0.7 all-gather.5.cloned.1.call-update
  7.9 0.0 all-gather.3.cloned.1.call-start
  8.0 0.9 fusion.16
  8.8 0.8 fusion.18
  9.7 0.6 copy.10
  10.3 0.0 all-gather.3.cloned.1.call-update
  10.3 0.0 reduce-scatter.2.cloned.1.call-start
  10.4 0.8 reduce-window.8
  11.2 0.1 pad_add_fusion
  11.3 0.0 copy-start.1
  11.3 29.7 %all-gather.5.cloned.1.call-done = bf16[4096,512]{1,0:T(8,128)(2,1)} async-done(((bf16[2048,512]{1,0:T(8,128)(2,1)}), bf16[4096,512]{1,0:T(8,128)(2,1)}) %all-gather.5.cloned.1.call-update) | async-done | bytes 4194320 | tf_op jit(solution)/shard_map/all_gather | solution.py:41
  41.0 216.8 %all-gather.3.cloned.1.call-done = bf16[1,512,4096]{2,0,1:T(2,128)(2,1)} async-done(((bf16[1,2,4096]{2,0,1:T(2,128)(2,1)}), bf16[1,512,4096]{2,0,1:T(2,128)(2,1)}) %all-gather.3.cloned.1.call-update) | async-done | bytes 4194320 | tf_op jit(solution)/shard_map/all_gather | solution.py:68
  257.8 9.3 %fusion.1 = f32[512,512]{1,0:T(8,128)S(1)} fusion(bf16[4096,512]{1,0:T(8,128)(2,1)} %all-gather.5.cloned.1.call-done, bf16[1,512,4096]{2,0,1:T(2,128)(2,1)} %all-gather.3.cloned.1.call-done), kind=kOutput, calls=%fused_computation.2 | convolution fusion | flops 2147483648 | bytes 9437184 | tf_op jit(solution)/shard_map/dot_general | solution.py:52
  267.1 1.4 fusion.7
  268.5 11.3 %psum.21 = f32[8,512]{1,0:T(8,128)S(1)} all-reduce(f32[8,512]{1,0:T(8,128)S(1)} %fusion.7), channel_id=1, replica_groups=mesh['dp'=64,'segment'=2,'mp'=4] {'segment'}, use_global_device_ids=true, to_apply=%region_2.3 | all-reduce | flops 4096 | bytes 32768 | tf_op jit(solution)/shard_map/psum | solution.py:56
  279.7 0.0 copy-done
  279.7 0.1 convolution_bitcast_fusion
  279.9 115.1 %psum.22 = f32[8,8]{0,1:T(8,128)S(1)} all-reduce(f32[8,8]{0,1:T(8,128)S(1)} %convolution_bitcast_fusion), channel_id=1, replica_groups=mesh['dp'=64,'segment'=2,'mp'=4] {'dp'}, use_global_device_ids=true, to_apply=%region_3.4 | all-reduce | flops 64 | bytes 512 | tf_op jit(solution)/shard_map/psum | solution.py:58
  395.0 6.3 %psum.23 = f32[8,8]{0,1:T(8,128)S(1)} all-reduce(f32[8,8]{0,1:T(8,128)S(1)} %psum.22), channel_id=1, replica_groups=mesh['dp'=64,'segment'=2,'mp'=4] {'mp'}, use_global_device_ids=true, to_apply=%region_4.5 | all-reduce | flops 64 | bytes 512 | tf_op jit(solution)/shard_map/psum | solution.py:58
  401.4 0.0 copy-done.1
  401.4 0.6 subtract_reduce_fusion
  402.0 0.1 convolution_multiply_fusion.1
  402.1 1.4 fusion.6
  403.5 14.9 %convolution_convert_fusion = bf16[4096,512]{1,0:T(8,128)(2,1)} fusion(bf16[512,512]{1,0:T(8,128)(2,1)S(1)} %fusion.6, bf16[1,512,4096]{2,0,1:T(2,128)(2,1)} %all-gather.3.cloned.1.call-done), kind=kOutput, calls=%fused_computation | convolution fusion | flops 2149580800 | bytes 8912896 | tf_op jit(solution)/shard_map/dot_general | solution.py:69
  418.4 0.0 reduce-scatter.2.cloned.1.call-update
  418.4 40.0 %reduce-scatter.2.cloned.1.call-done = bf16[2048,512]{1,0:T(8,128)(2,1)} async-done(((bf16[4096,512]{1,0:T(8,128)(2,1)}), bf16[2048,512]{1,0:T(8,128)(2,1)}) %reduce-scatter.2.cloned.1.call-update) | async-done | bytes 2097168 | tf_op jit(solution)/shard_map/reduce_scatter | solution.py:72
  (4 shorter events, 0.1 us)
Async XLA Ops:
  7.2 272.6 %copy-start = (bf16[8,512]{1,0:T(8,128)(2,1)S(1)}, bf16[8,512]{1,0:T(8,128)(2,1)}, u32[]{:S(2)}) copy-start(bf16[8,512]{1,0:T(8,128)(2,1)} %param.9) | copy-start | bytes 24580
  7.2 33.8 %all-gather.5.cloned.1.call-start = ((), (), s32[]{:S(2)}) async-start(), calls=%async_computation.2 | async-start | bytes 6291456 | tf_op jit(solution)/shard_map/all_gather | solution.py:41
  7.9 249.9 %all-gather.3.cloned.1.call-start = ((), (), s32[]{:S(2)}) async-start(), calls=%async_computation.1 | async-start | bytes 8421376 | tf_op jit(solution)/shard_map/all_gather | solution.py:68
  10.3 448.1 %reduce-scatter.2.cloned.1.call-start = ((), (), s32[]{:S(2)}) async-start(), calls=%async_computation.3 | async-start | bytes 6291456 | tf_op jit(solution)/shard_map/reduce_scatter | solution.py:72
  11.3 390.0 %copy-start.1 = (s32[8]{0:T(128)S(1)}, s32[8]{0:T(128)}, u32[]{:S(2)}) copy-start(s32[8]{0:T(128)} %param.11) | copy-start | bytes 100
Sparse Core Ops, SparseCore 0:
  10.1 30.8 all-gather.4
  46.2 211.6 all-gather.2
  418.5 39.8 reduce-scatter.1
